TPU v7x, 256 devices: a whole 4x4x8 slice. The times are simulated.
256 devices in a mesh: cells: 8 (over x, core), genes: 32 (over z, y).
Axes of the slice: x: 4, y: 4, z: 8, core: 2. Of those that a mesh axis runs over, the one named last changes fastest.
Arguments:
- expression: bfloat16 [16384, 61440], P('cells', 'genes'), may hold values from -6 to 6
- labels: int32 [16384], P('cells'), may hold values from 0 to 255, as said below
Outputs:
- welch_t: float32 [256, 61440], P(('cells', 'genes'))
- fold_change: float32 [256, 61440], P(('cells', 'genes'))
Inputs may be any that keep to these rules, and one draw needn't show every extreme that they name: `labels`: every cluster holds at least two cells.
All inputs are finite; a program needn't handle non-finite values.
Results may differ from a plain program's by a relative error of at most 0.0003.
Values sent between devices are 32-bit elements; how exact they have to be, the bound alone decides.
A program may use at most 64 MiB of HBM per device.

v0:
```python
import jax
import jax.numpy as jnp
from jax import lax
from jax.sharding import PartitionSpec as P

K = 256


def welch(sums, squares, sizes, total_sum, total_squares, cells_all):
    mean_in = sums / sizes
    var_in = jnp.maximum((squares - sums * mean_in) / (sizes - 1.0), 0.1)
    rest = cells_all - sizes
    rest_sum = total_sum - sums
    mean_out = rest_sum / rest
    var_out = jnp.maximum((total_squares - squares - rest_sum * mean_out) / (rest - 1.0), 0.1)
    fold = mean_in - mean_out
    return (fold / jnp.sqrt(var_in / sizes + var_out / rest), fold)


def on_device(expression, labels):
    cell_dev, gene_block = expression.shape
    slabs = lax.axis_size("cells")
    cells_all = jnp.float32(cell_dev * slabs)
    cluster_ids = jnp.arange(K, dtype=jnp.int32)
    member = (cluster_ids[:, None] == labels[None, :]).astype(jnp.bfloat16)
    member_wide = member.astype(jnp.float32)
    values_wide = expression.astype(jnp.float32)
    squared = values_wide * values_wide
    highest = lax.Precision.HIGHEST
    sizes = lax.psum(jnp.sum(member, axis=1, dtype=jnp.float32), "cells")
    sizes = sizes[:, None]
    dims = (((0,), (1,)), ((), ()))
    first = lax.dot_general(expression, member, dims, preferred_element_type=jnp.float32)
    second = lax.dot_general(
        squared, member_wide, dims, precision=highest, preferred_element_type=jnp.float32
    )
    reduced = lax.psum_scatter(
        jnp.concatenate([first, second], axis=1), "cells", scatter_dimension=0, tiled=True
    )
    reduced = jnp.transpose(reduced)
    sums = reduced[:K]
    squares = reduced[K:]
    total_sum = jnp.sum(sums, axis=0, keepdims=True)
    total_squares = jnp.sum(squares, axis=0, keepdims=True)
    welch_t, fold = welch(sums, squares, sizes, total_sum, total_squares, cells_all)
    welch_t, fold = (
        lax.all_to_all(
            lax.all_to_all(welch_t, "cells", split_axis=0, concat_axis=1, tiled=True),
            "genes",
            split_axis=0,
            concat_axis=1,
            tiled=True,
        ),
        lax.all_to_all(
            lax.all_to_all(fold, "cells", split_axis=0, concat_axis=1, tiled=True),
            "genes",
            split_axis=0,
            concat_axis=1,
            tiled=True,
        ),
    )
    return (welch_t, fold)


def solution(mesh):
    return jax.shard_map(
        on_device,
        mesh=mesh,
        in_specs=(P("cells", "genes"), P("cells")),
        out_specs=(P(("cells", "genes"), None), P(("cells", "genes"), None)),
        check_vma=False,
    )
```

profile of v0, /device:TPU:1, one launch (start us, length us, event | category | flops | bytes accessed | tf_op | source)
XLA Modules:
  0.0 140.5 jit_solution(4590700866040163208)
XLA Ops:
  7.2 0.0 copy-start
  7.2 0.0 reduce-scatter.4.cloned.1.call-start
  7.2 0.0 copy-start.1
  7.2 13.1 %fusion = f32[1920,256]{0,1:T(8,128)S(1)} fusion(bf16[2048,1920]{1,0:T(8,128)(2,1)} %param.2, s32[2048]{0:T(1024)} %param.3), kind=kOutput, calls=%fused_computation | convolution fusion | flops 12087984128 | bytes 9838592 | tf_op jit(solution)/shard_map/dot_general | solution.py:34
  20.3 0.0 copy-done
  20.3 0.0 copy-done.1
  20.3 2.4 %convolution_bitcast_fusion = f32[1920,256]{0,1:T(8,128)S(1)} fusion(bf16[2048,1920]{1,0:T(8,128)(2,1)S(1)} %copy-done.1, s32[2048]{0:T(1024)S(1)} %copy-done), kind=kOutput, calls=%fused_computation.4 | convolution fusion | flops 2013790208 | bytes 9838592 | tf_op jit(solution)/shard_map/dot_general | solution.py:33
  22.7 2.2 %pad_maximum_fusion = f32[1920,512]{0,1:T(8,128)} fusion(f32[1920,256]{0,1:T(8,128)S(1)} %fusion, f32[1920,256]{0,1:T(8,128)S(1)} %convolution_bitcast_fusion), kind=kLoop, calls=%fused_computation.3 | loop fusion | flops 983040 | bytes 7864320 | tf_op jit(solution)/shard_map/concatenate | solution.py:38
  24.9 5.5 %copy.14 = f32[1920,512]{1,0:T(8,128)} copy(f32[1920,512]{0,1:T(8,128)} %pad_maximum_fusion) | data formatting | bytes 7864320
  30.4 0.0 reduce-scatter.4.cloned.1.call-update
  30.4 0.3 convert_reduce_fusion
  30.7 15.0 %psum.7 = f32[256]{0:T(256)S(1)} all-reduce(f32[256]{0:T(256)S(1)} %convert_reduce_fusion), channel_id=1, replica_groups=mesh['cells'=8,'genes'=32] {'cells'}, use_global_device_ids=true, to_apply=%region_2.0 | all-reduce | flops 256 | bytes 2048 | tf_op jit(solution)/shard_map/psum | solution.py:30
  45.7 25.7 %reduce-scatter.4.cloned.1.call-done = f32[240,512]{1,0:T(8,128)} async-done(((f32[1920,512]{1,0:T(8,128)}), f32[240,512]{1,0:T(8,128)}) %reduce-scatter.4.cloned.1.call-update) | async-done | bytes 491536
  71.4 1.2 copy.15
  72.6 0.1 slice_reduce_fusion.1
  72.7 1.0 divide_subtract_fusion
  73.6 12.5 %all_to_all.66 = f32[8,32,240]{2,1,0:T(8,128)S(1)} all-to-all(f32[8,32,240]{2,1,0:T(8,128)S(1)} %bitcast.15), channel_id=1, replica_groups=mesh['cells'=8,'genes'=32] {'cells'}, dimensions={0} | all-to-all | bytes 491520 | tf_op jit(solution)/shard_map/all_to_all | solution.py:48
  86.1 4.4 %all-to-all-start.2 = ((f32[8,32,240]{2,1,0:T(8,128)}), f32[8,32,240]{2,1,0:T(8,128)S(1)}, u32[]{:S(2)}, u32[]{:S(2)}) async-start(f32[8,32,240]{2,1,0:T(8,128)} %bitcast.5), calls=%async_computation.2 | async-start | bytes 524288 | tf_op jit(solution)/shard_map/all_to_all | solution.py:55
  90.5 0.2 copy.10
  90.7 1.1 all_to_all.60
  91.8 5.2 %all-to-all-done.2 = f32[8,32,240]{2,1,0:T(8,128)S(1)} async-done(((f32[8,32,240]{2,1,0:T(8,128)}), f32[8,32,240]{2,1,0:T(8,128)S(1)}, u32[]{:S(2)}, u32[]{:S(2)}) %all-to-all-start.2) | async-done | bytes 245792 | tf_op jit(solution)/shard_map/all_to_all | solution.py:55
  97.0 9.5 %all-to-all-start.1 = ((f32[32,1,1920]{2,1,0:T(1,128)}), f32[32,1,1920]{2,1,0:T(1,128)S(1)}, u32[]{:S(2)}, u32[]{:S(2)}) async-start(f32[32,1,1920]{2,1,0:T(1,128)} %all_to_all.60), calls=%async_computation.1 | async-start | bytes 491520 | tf_op jit(solution)/shard_map/all_to_all | solution.py:47
  106.6 0.2 copy.12
  106.7 1.1 all_to_all.61
  107.9 9.1 %all-to-all-done.1 = f32[32,1,1920]{2,1,0:T(1,128)S(1)} async-done(((f32[32,1,1920]{2,1,0:T(1,128)}), f32[32,1,1920]{2,1,0:T(1,128)S(1)}, u32[]{:S(2)}, u32[]{:S(2)}) %all-to-all-start.1) | async-done | bytes 245792 | tf_op jit(solution)/shard_map/all_to_all | solution.py:47
  116.9 5.1 %all-to-all-start.3 = ((f32[32,1,1920]{2,1,0:T(1,128)}), f32[32,1,1920]{2,1,0:T(1,128)S(1)}, u32[]{:S(2)}, u32[]{:S(2)}) async-start(f32[32,1,1920]{2,1,0:T(1,128)} %all_to_all.61), calls=%async_computation.3 | async-start | bytes 491520 | tf_op jit(solution)/shard_map/all_to_all | solution.py:54
  122.0 10.3 %all-to-all-done.3 = f32[32,1,1920]{2,1,0:T(1,128)S(1)} async-done(((f32[32,1,1920]{2,1,0:T(1,128)}), f32[32,1,1920]{2,1,0:T(1,128)S(1)}, u32[]{:S(2)}, u32[]{:S(2)}) %all-to-all-start.3) | async-done | bytes 245792 | tf_op jit(solution)/shard_map/all_to_all | solution.py:54
  132.3 0.7 copy.18
  133.0 0.7 copy.19
  (1 shorter events, 0.0 us)
Async XLA Ops:
  7.2 13.1 %copy-start = (s32[2048]{0:T(1024)S(1)}, s32[2048]{0:T(1024)}, u32[]{:S(2)}) copy-start(s32[2048]{0:T(1024)} %param.3) | copy-start | bytes 24580
  7.2 64.2 %reduce-scatter.4.cloned.1.call-start = ((), (), s32[]{:S(2)}) async-start(), calls=%async_computation.5 | async-start | bytes 4423680
  7.2 13.1 %copy-start.1 = (bf16[2048,1920]{1,0:T(8,128)(2,1)S(1)}, bf16[2048,1920]{1,0:T(8,128)(2,1)}, u32[]{:S(2)}) copy-start(bf16[2048,1920]{1,0:T(8,128)(2,1)} %param.2) | copy-start | bytes 23592964
  86.1 10.9 %all-to-all-start.2 = ((f32[8,32,240]{2,1,0:T(8,128)}), f32[8,32,240]{2,1,0:T(8,128)S(1)}, u32[]{:S(2)}, u32[]{:S(2)}) async-start(f32[8,32,240]{2,1,0:T(8,128)} %bitcast.5), calls=%async_computation.2 | async-start | bytes 524288 | tf_op jit(solution)/shard_map/all_to_all | solution.py:55
  97.0 19.9 %all-to-all-start.1 = ((f32[32,1,1920]{2,1,0:T(1,128)}), f32[32,1,1920]{2,1,0:T(1,128)S(1)}, u32[]{:S(2)}, u32[]{:S(2)}) async-start(f32[32,1,1920]{2,1,0:T(1,128)} %all_to_all.60), calls=%async_computation.1 | async-start | bytes 491520 | tf_op jit(solution)/shard_map/all_to_all | solution.py:47
  116.9 15.4 %all-to-all-start.3 = ((f32[32,1,1920]{2,1,0:T(1,128)}), f32[32,1,1920]{2,1,0:T(1,128)S(1)}, u32[]{:S(2)}, u32[]{:S(2)}) async-start(f32[32,1,1920]{2,1,0:T(1,128)} %all_to_all.61), calls=%async_computation.3 | async-start | bytes 491520 | tf_op jit(solution)/shard_map/all_to_all | solution.py:54
Sparse Core Ops, SparseCore 0:
  30.5 40.8 reduce-scatter.3
where the time goes:
time: 142 us; the launch traced here: 141 us
  waiting for transfers between devices  50.3 us (35%)
  blocking collectives  27.5 us (19%)
  starting transfers between devices  19 us (13%)
  matrix products  15.5 us (11%)
  between operations  14.1 us (10%)
  local copies, waits for them, and re-layouts  10.7 us (8%)
  other arithmetic  3.46 us (2%)
    unnamed x2, waiting for transfers between devices  25.7 us
    psum x1, blocking collectives, on_device(): sizes = lax.psum(jnp.sum(member, axis=1, dtype=jnp.float32), 'cells')  15 us
    dot_general x1, matrix products, on_device(): lax.dot_general(squared, member_wide, dims, precision=highest, preferred_...  13.1 us
    all_to_all x1, blocking collectives, on_device(): lax.all_to_all(welch_t, 'cells', split_axis=0, concat_axis=1, tiled=True)  12.5 us
    all_to_all x1, waiting for transfers between devices, on_device(): lax.all_to_all(lax.all_to_all(fold, 'cells', split_axis=0, concat_axis=1,...  10.3 us
    all_to_all x1, starting transfers between devices, on_device(): lax.all_to_all(lax.all_to_all(welch_t, 'cells', split_axis=0, concat_axis...  9.53 us
    all_to_all x1, waiting for transfers between devices, on_device(): lax.all_to_all(lax.all_to_all(welch_t, 'cells', split_axis=0, concat_axis...  9.06 us
    unnamed x8, local copies, waits for them, and re-layouts  8.09 us
  transfers between devices with their start and end apart: 4, of which 4 were waited for; matrix products, arithmetic and copies ran while one was open for 0% of the time, Pallas kernels for 0%

commit v1 on v0

v1 whole, which is shorter than its diff:
```python
import functools

import jax
import jax.numpy as jnp
from jax import lax
from jax.experimental import pallas as pl
from jax.experimental.pallas import tpu as pltpu
from jax.sharding import PartitionSpec as P

MESH = pl.DeviceIdType.MESH
LANES = 128
CHIPS = 4
SLABS = (4, 4, 4, 3)


def welch(sums, squares, total_sum, total_squares, sizes, cells_all):
    mean_in = sums / sizes
    var_in = jnp.maximum((squares - sums * mean_in) / (sizes - 1.0), 0.1)
    rest = cells_all - sizes
    rest_sum = total_sum - sums
    mean_out = rest_sum / rest
    var_out = jnp.maximum((total_squares - squares - rest_sum * mean_out) / (rest - 1.0), 0.1)
    fold = mean_in - mean_out
    return fold / jnp.sqrt(var_in / sizes + var_out / rest), fold


def kernel(slabs, labels_ref, x_ref, t_ref, f_ref, xv, member, lab, row_t, row_f, part, pair, hop, final, *sems):
    (load_sem, pair_send, pair_recv, hop_send, hop_recv, early_send, early_recv, late_send, late_recv,
     lab_send, lab_recv, row_send, row_recv) = sems
    n = len(slabs)
    starts = [sum(slabs[:j]) for j in range(n)]
    clusters, cell_dev = member.shape
    lab_rows = labels_ref.shape[0]
    own = row_t.shape[0]
    genes = row_t.shape[2]
    cells_all = jnp.float32(cell_dev * 2 * CHIPS)

    me = lax.axis_index("cells")
    g = lax.axis_index("genes")
    chip, core = me // 2, me % 2
    right, left, across = (chip + 1) % CHIPS, (chip + 3) % CHIPS, (chip + 2) % CHIPS

    def at_cells(index):
        return {"cells": index, "genes": g}

    def at_genes(index):
        return {"cells": me, "genes": index}

    loads = []
    for j in range(n):
        cols = pl.ds(starts[j] * LANES, slabs[j] * LANES)
        loads.append(pltpu.make_async_copy(x_ref.at[:, cols], xv.at[:, cols], load_sem.at[j]))
        loads[j].start()

    barrier = pltpu.get_barrier_semaphore()
    for d in range(1, 2 * CHIPS):
        pl.semaphore_signal(barrier, inc=1, device_id=at_cells((me + d) % (2 * CHIPS)), device_id_type=MESH)

    @pl.loop(1, own)
    def _(d):
        pl.semaphore_signal(barrier, inc=1, device_id=at_genes((g + d) % own), device_id_type=MESH)

    ids = lax.broadcasted_iota(jnp.int32, (clusters, LANES), 0)
    for r in range(cell_dev // LANES):
        member[:, r * LANES:(r + 1) * LANES] = (ids == labels_ref[r:r + 1, :]).astype(jnp.float32).astype(jnp.bfloat16)

    def rows_of(j):
        return slabs[j] * own

    def compute(j):
        base = starts[j]
        tot = [[], []]
        for s0 in range(0, slabs[j], 2):
            width = min(2, slabs[j] - s0)
            cols = slice((base + s0) * LANES, (base + s0 + width) * LANES)
            x = xv[:, cols]
            wide = x.astype(jnp.float32)
            wide = wide * wide
            high = wide.astype(jnp.bfloat16)
            low = (wide - high.astype(jnp.float32)).astype(jnp.bfloat16)
            m = member[...]
            first = jnp.dot(m, x, preferred_element_type=jnp.float32)
            second = jnp.dot(m, high, preferred_element_type=jnp.float32)
            second += jnp.dot(m, low, preferred_element_type=jnp.float32)
            for kind, res in enumerate((first, second)):
                for w in range(width):
                    piece = res[:, w * LANES:(w + 1) * LANES]
                    s = s0 + w
                    for d in range(2 * CHIPS):
                        part[j][d % 2, d // 2, kind, s * own:(s + 1) * own, :] = piece[d * own:(d + 1) * own, :]
                    tot[kind].append(jnp.sum(piece, axis=0, keepdims=True))
        line = lax.broadcasted_iota(jnp.int32, (8, LANES), 0)
        for kind in range(2):
            block = jnp.zeros((8, LANES), jnp.float32)
            for s in range(slabs[j]):
                block = jnp.where(line == s, tot[kind][s], block)
            for d in range(2 * CHIPS):
                part[j][d % 2, d // 2, kind, rows_of(j):, :] = block

    def remote(src, dst, send, recv, device):
        copy = pltpu.make_async_remote_copy(
            src_ref=src, dst_ref=dst, send_sem=send, recv_sem=recv, device_id=device, device_id_type=MESH
        )
        copy.start()
        return copy

    sent = []

    def share(j):
        copy = remote(part[j].at[1 - core], pair[j], pair_send.at[j], pair_recv.at[j], at_cells(2 * chip + 1 - core))
        sent.append(copy)
        return copy

    def start_x(j, copy):
        copy.wait_recv()
        pair[j][...] += part[j][core]
        copies = []
        for side, to in enumerate((right, left)):
            device = at_cells(2 * to + core)
            copies.append(remote(pair[j].at[across, side], hop[j].at[side], hop_send.at[j, side], hop_recv.at[j, side], device))
            copies.append(remote(pair[j].at[to, 1 - side], final[j].at[side, 1 - side],
                                 early_send.at[j, side], early_recv.at[j, side], device))
        sent.extend(copies)
        return copies

    def forward_x(j, copies):
        out = [copies[1], copies[3]]
        for side, to in enumerate((right, left)):
            copies[2 * side].wait_recv()
            pair[j][to, side] += hop[j][side]
            out.append(remote(pair[j].at[to, side], final[j].at[side, side],
                              late_send.at[j, side], late_recv.at[j, side], at_cells(2 * to + core)))
        sent.extend(out[2:])
        return out

    def finish(j, copies, sizes):
        for copy in copies:
            copy.wait_recv()
        mine = [pair[j][chip, kind] + final[j][0, kind] + final[j][1, kind] for kind in range(2)]
        for s in range(slabs[j]):
            sums, squares = (mine[kind][s * own:(s + 1) * own] for kind in range(2))
            total_sum, total_squares = (mine[kind][rows_of(j) + s:rows_of(j) + s + 1] for kind in range(2))
            t, fold = welch(sums, squares, total_sum, total_squares, sizes, cells_all)
            cols = pl.ds((starts[j] + s) * LANES, LANES)
            row_t[:, :, cols] = t.reshape(own, 1, LANES)
            row_f[:, :, cols] = fold.reshape(own, 1, LANES)
        cols = pl.ds(starts[j] * LANES, slabs[j] * LANES)
        place = pl.ds(pl.multiple_of(g * genes + starts[j] * LANES, LANES), slabs[j] * LANES)

        @pl.loop(1, own)
        def _(d):
            to = (g + d) % own
            for kind, (row, out) in enumerate(((row_t, t_ref), (row_f, f_ref))):
                remote(row.at[to, :, cols], out.at[:, place], row_send.at[kind], row_recv.at[kind], at_genes(to))

        for kind, (row, out) in enumerate(((row_t, t_ref), (row_f, f_ref))):
            pltpu.make_async_copy(row.at[g, :, cols], out.at[:, place], row_recv.at[kind]).start()

    def count():
        for d in range(1, 2 * CHIPS):
            slot = (me + 2 * CHIPS - d) % (2 * CHIPS)
            pltpu.make_async_copy(lab.at[slot], lab.at[slot], lab_recv.at[d]).wait()
        mine = lax.broadcasted_iota(jnp.int32, (own, LANES), 0) + me * own
        counts = jnp.zeros((own, LANES), jnp.float32)
        for d in range(2 * CHIPS):
            for r in range(lab_rows):
                counts += (mine == lab[d, r:r + 1, :]).astype(jnp.float32)
        return jnp.sum(counts, axis=1, keepdims=True)

    pairs, hops, lates = [None] * n, [None] * n, [None] * n
    for j in range(n):
        loads[j].wait()
        compute(j)
        if j == 0:
            pl.semaphore_wait(barrier, 2 * CHIPS - 1 + own - 1)
        pairs[j] = share(j)
        if j == 0:
            for d in range(1, 2 * CHIPS):
                sent.append(remote(labels_ref, lab.at[me], lab_send.at[d], lab_recv.at[d],
                                   at_cells((me + d) % (2 * CHIPS))))
            lab[me] = labels_ref[...]
        if j >= 1:
            hops[j - 1] = start_x(j - 1, pairs[j - 1])
        if j >= 2:
            lates[j - 2] = forward_x(j - 2, hops[j - 2])
    sizes = count()
    hops[n - 1] = start_x(n - 1, pairs[n - 1])
    for j in range(n):
        if lates[j] is None:
            lates[j] = forward_x(j, hops[j])
        if j >= 1:
            finish(j - 1, lates[j - 1], sizes)
    finish(n - 1, lates[n - 1], sizes)

    for copy in sent:
        copy.wait_send()
    for kind, (row, out) in enumerate(((row_t, t_ref), (row_f, f_ref))):
        others = row.at[pl.ds(0, own - 1)]
        pltpu.make_async_copy(others, others, row_send.at[kind]).wait()
        pltpu.make_async_copy(out, out, row_recv.at[kind]).wait()


def on_device(slabs, clusters, expression, labels):
    cell_dev, genes = expression.shape
    own = lax.axis_size("genes")
    n = len(slabs)
    f32 = jnp.float32
    rows = [s * own + 8 for s in slabs]
    dma = pltpu.SemaphoreType.DMA
    line = jax.ShapeDtypeStruct((1, genes * own), f32)
    return pl.pallas_call(
        functools.partial(kernel, slabs),
        out_shape=(line, line),
        in_specs=[pl.BlockSpec(memory_space=pltpu.VMEM), pl.BlockSpec(memory_space=pl.ANY)],
        out_specs=(pl.BlockSpec(memory_space=pl.ANY),) * 2,
        scratch_shapes=[
            pltpu.VMEM((cell_dev, genes), jnp.bfloat16),
            pltpu.VMEM((clusters, cell_dev), jnp.bfloat16),
            pltpu.VMEM((2 * CHIPS, cell_dev // LANES, LANES), jnp.int32),
            pltpu.VMEM((own, 1, genes), f32),
            pltpu.VMEM((own, 1, genes), f32),
            [pltpu.VMEM((2, CHIPS, 2, r, LANES), f32) for r in rows],
            [pltpu.VMEM((CHIPS, 2, r, LANES), f32) for r in rows],
            [pltpu.VMEM((2, r, LANES), f32) for r in rows],
            [pltpu.VMEM((2, 2, r, LANES), f32) for r in rows],
            dma((n,)),
            dma((n,)), dma((n,)),
            dma((n, 2)), dma((n, 2)),
            dma((n, 2)), dma((n, 2)),
            dma((n, 2)), dma((n, 2)),
            dma((2 * CHIPS,)), dma((2 * CHIPS,)),
            dma((2,)), dma((2,)),
        ],
        compiler_params=pltpu.CompilerParams(
            collective_id=0, has_side_effects=True, vmem_limit_bytes=56 * 1024 * 1024
        ),
    )(labels.reshape(cell_dev // LANES, LANES), expression)


def solution(mesh):
    clusters = mesh.shape["cells"] * mesh.shape["genes"]
    return jax.shard_map(
        functools.partial(on_device, SLABS, clusters),
        mesh=mesh,
        in_specs=(P("cells", "genes"), P("cells")),
        out_specs=(P(("cells", "genes"), None), P(("cells", "genes"), None)),
        check_vma=False,
    )
```

time: 142 us -> 44.7 us (0.31)
  waiting for transfers between devices: 50.3 us -> 0 us
  Pallas kernels: 0 us -> 40.1 us
  blocking collectives: 27.5 us -> 0 us
  starting transfers between devices: 19 us -> 0 us
  matrix products: 15.5 us -> 0 us
  between operations: 14.1 us -> 0.64 us
  local copies, waits for them, and re-layouts: 10.7 us -> 3.31 us
  other arithmetic: 3.46 us -> 0 us
    pallas_call x0 -> x1, Pallas kernels: none -> 40.1 us  [on_device(): pl.pallas_call(functools.partial(kernel, slabs), out_shape=(line, line),...]
    unnamed x2 -> x0, waiting for transfers between devices: 25.7 us -> none
    all_to_all x3 -> x0, waiting for transfers between devices: 24.6 us -> none  [the longest x1 10.3 us: on_device(): lax.all_to_all(lax.all_to_all(fold, 'cells', split_axis=0, concat_axis=1,...]
    all_to_all x3 -> x0, starting transfers between devices: 19 us -> none  [the longest x1 9.53 us: on_device(): lax.all_to_all(lax.all_to_all(welch_t, 'cells', split_axis=0, concat_axis...]
    dot_general x2 -> x0, matrix products: 15.5 us -> none  [the longest x1 13.1 us: on_device(): lax.dot_general(squared, member_wide, dims, precision=highest, preferred_...]
    psum x1 -> x0, blocking collectives: 15 us -> none  [on_device(): sizes = lax.psum(jnp.sum(member, axis=1, dtype=jnp.float32), 'cells')]
    all_to_all x1 -> x0, blocking collectives: 12.5 us -> none  [on_device(): lax.all_to_all(welch_t, 'cells', split_axis=0, concat_axis=1, tiled=True)]
    unnamed x8 -> x2, local copies, waits for them, and re-layouts: 8.09 us -> 3.31 us
  transfers between devices with their start and end apart: 4 -> 0, of which waited for: 4 -> 0; matrix products, arithmetic and copies ran while one was open for 0% -> 0% of each run, Pallas kernels for 0% -> 0%
where the time goes in v1:
time: 44.7 us; the launch traced here: 44 us
  Pallas kernels  40.1 us (90%)
  local copies, waits for them, and re-layouts  3.31 us (7%)
  between operations  0.64 us (1%)
    pallas_call x1, Pallas kernels, on_device(): pl.pallas_call(functools.partial(kernel, slabs), out_shape=(line, line),...  40.1 us
    unnamed x2, local copies, waits for them, and re-layouts  3.31 us

profile of v1, /device:TPU:1, one launch (start us, length us, event | category | flops | bytes accessed | tf_op | source)
XLA Modules:
  0.0 44.0 jit_solution(10506610320828642917)
XLA Ops:
  0.6 40.1 %shard_map.41 = (f32[1,61440]{1,0:T(1,128)}, f32[1,61440]{1,0:T(1,128)}) custom-call(s32[16,128]{1,0:T(8,128)} %bitcast.1, bf16[2048,1920]{1,0:T(8,128)(2,1)} %x_ref.1), custom_call_target="tpu_custom_call" | custom-call | tf_op jit(solution)/shard_map/pallas_call | solution.py:211
  40.7 1.7 %copy.6 = f32[1,61440]{1,0:T(1,128)} copy(f32[1,61440]{1,0:T(1,128)} %get-tuple-element.4) | data formatting | bytes 491520
  42.4 1.7 %copy.7 = f32[1,61440]{1,0:T(1,128)} copy(f32[1,61440]{1,0:T(1,128)} %get-tuple-element.5) | data formatting | bytes 491520

commit v2 on v1

v2 whole, which is shorter than its diff:
```python
import functools

import jax
import jax.numpy as jnp
from jax import lax
from jax.experimental import pallas as pl
from jax.experimental.pallas import tpu as pltpu
from jax.sharding import PartitionSpec as P

MESH = pl.DeviceIdType.MESH
LANES = 128
CHIPS = 4
SLABS = (4, 4, 4, 3)
NY = 4
EXTRA = 16
EAGER, LAG = False, 1
SPAN = 4
ROWS_AFTER = (0, 1, 2, 3)


def kernel(slabs, labels_ref, x_ref, y_ref, xv, member, lab, row, tot_own, tot_pair, tot_chip,
           part, pair, hop, final, load_sem, pair_recv, hop_recv, final_recv, tot_recv, all_recv,
           pair_send, x_send, tot_send, all_send, lab_send, lab_recv, row_send, row_recv):
    n = len(slabs)
    starts = [sum(slabs[:j]) for j in range(n)]
    clusters, cell_dev = member.shape[0] - EXTRA, member.shape[1]
    lab_rows = labels_ref.shape[0]
    own = row.shape[0]
    cells_all = jnp.float32(cell_dev * 2 * CHIPS)

    me = lax.axis_index("cells")
    g = lax.axis_index("genes")
    chip, core = me // 2, me % 2
    right, left, across = (chip + 1) % CHIPS, (chip + 3) % CHIPS, (chip + 2) % CHIPS

    def at_cells(index):
        return {"cells": index, "genes": g}

    def at_genes(index):
        return {"cells": me, "genes": index}

    loads = []
    for j in range(n):
        cols = pl.ds(starts[j] * LANES, slabs[j] * LANES)
        loads.append(pltpu.make_async_copy(x_ref.at[:, cols], xv.at[:, cols], load_sem.at[j]))
        loads[j].start()

    barrier = pltpu.get_barrier_semaphore()
    for d in range(1, 2 * CHIPS):
        pl.semaphore_signal(barrier, inc=1, device_id=at_cells((me + d) % (2 * CHIPS)), device_id_type=MESH)

    peers = {}
    for far in range(own // NY):
        level = lax.rem(lax.div(g, NY) + far, own // NY) * NY
        for d in range(0 if far else 1, NY):
            peers[far, d] = level + lax.rem(g + d, NY)
            pl.semaphore_signal(barrier, inc=1, device_id=at_genes(peers[far, d]), device_id_type=MESH)

    ids = lax.broadcasted_iota(jnp.int32, (clusters, LANES), 0)
    for r in range(cell_dev // LANES):
        hits = (ids == labels_ref[r:r + 1, :]).astype(jnp.float32).astype(jnp.bfloat16)
        member[:clusters, r * LANES:(r + 1) * LANES] = hits
    member[clusters:, :] = jnp.ones((EXTRA, cell_dev), jnp.bfloat16)
    tot_own[...] = jnp.zeros_like(tot_own)

    def rows_of(j):
        return pl.ds(starts[j] * own, slabs[j] * own)

    def compute(j):
        for s0 in range(0, slabs[j], 2):
            width = min(2, slabs[j] - s0)
            base = starts[j] + s0
            x = xv[:, base * LANES:(base + width) * LANES]
            wide = x.astype(jnp.float32)
            wide = wide * wide
            high = wide.astype(jnp.bfloat16)
            low = (wide - high.astype(jnp.float32)).astype(jnp.bfloat16)
            m = member[...]
            first = jnp.dot(m, x, preferred_element_type=jnp.float32)
            second = jnp.dot(m, high, preferred_element_type=jnp.float32)
            second += jnp.dot(m, low, preferred_element_type=jnp.float32)
            for kind, res in enumerate((first, second)):
                for w in range(width):
                    piece = res[:, w * LANES:(w + 1) * LANES]
                    s = base + w
                    for d in range(2 * CHIPS):
                        part[d % 2, d // 2, kind, s * own:(s + 1) * own, :] = piece[d * own:(d + 1) * own, :]
                    span, place = s // SPAN, s % SPAN + SPAN * kind
                    tot_own[span, place:place + 1, :] = piece[clusters:clusters + 1, :]

    def remote(src, dst, send, recv, device):
        pltpu.make_async_remote_copy(
            src_ref=src, dst_ref=dst, send_sem=send, recv_sem=recv, device_id=device, device_id_type=MESH
        ).start()

    def arrived(ref, sem):
        pltpu.make_async_copy(ref, ref, sem).wait()

    spans = {}
    for span in range(tot_own.shape[0]):
        last = min((span + 1) * SPAN, sum(slabs)) - 1
        j = max(j for j in range(n) if starts[j] <= last)
        spans.setdefault(j, []).append(span)

    def share(j):
        partner = at_cells(2 * chip + 1 - core)
        rows = rows_of(j)
        remote(part.at[1 - core, :, :, rows], pair.at[:, :, rows], pair_send, pair_recv.at[j], partner)
        for span in spans.get(j, ()):
            remote(tot_own.at[span], tot_pair.at[span], tot_send, tot_recv.at[span], partner)

    def start_x(j):
        rows = rows_of(j)
        arrived(pair.at[:, :, rows], pair_recv.at[j])
        pair[:, :, rows] += part[core, :, :, rows]
        for side, to in enumerate((right, left)):
            remote(pair.at[across, side, rows], hop.at[side, rows], x_send, hop_recv.at[j], at_cells(2 * to + core))
        for span in spans.get(j, ()):
            arrived(tot_pair.at[span], tot_recv.at[span])
            tot_chip[span, chip] = tot_own[span] + tot_pair[span]
            for d in (2, 1, 3):
                remote(tot_chip.at[span, chip], tot_chip.at[span, chip], all_send, all_recv.at[span],
                       at_cells((me + 2 * d) % (2 * CHIPS)))

    def early_x(j):
        rows = rows_of(j)
        for side, to in enumerate((right, left)):
            remote(pair.at[to, 1 - side, rows], final.at[side, 1 - side, rows], x_send, final_recv.at[j],
                   at_cells(2 * to + core))

    def forward_x(j):
        rows = rows_of(j)
        arrived(hop.at[:, rows], hop_recv.at[j])
        for side, to in enumerate((right, left)):
            pair[to, side, rows] += hop[side, rows]
            remote(pair.at[to, side, rows], final.at[side, side, rows], x_send, final_recv.at[j],
                   at_cells(2 * to + core))

    totals = {}
    rows_from = [0]

    def finish(j):
        rows = rows_of(j)
        arrived(final.at[:, :, rows], final_recv.at[j])
        rest = cells_all - sizes
        per_in, per_in_1, per_out, per_out_1 = 1.0 / sizes, 1.0 / (sizes - 1.0), 1.0 / rest, 1.0 / (rest - 1.0)
        mine = [pair[chip, kind, rows] + final[0, kind, rows] + final[1, kind, rows] for kind in range(2)]
        for s in range(slabs[j]):
            span, place = (starts[j] + s) // SPAN, (starts[j] + s) % SPAN
            if span not in totals:
                arrived(tot_chip.at[span, pl.ds(0, CHIPS - 1)], all_recv.at[span])
                totals[span] = (tot_chip[span, 0] + tot_chip[span, 1]) + (tot_chip[span, 2] + tot_chip[span, 3])
            total_sum = totals[span][place:place + 1]
            total_squares = totals[span][SPAN + place:SPAN + place + 1]
            sums, squares = (mine[kind][s * own:(s + 1) * own] for kind in range(2))
            mean_in = sums * per_in
            var_in = jnp.maximum((squares - sums * mean_in) * per_in_1, 0.1)
            rest_sum = total_sum - sums
            mean_out = rest_sum * per_out
            var_out = jnp.maximum((total_squares - squares - rest_sum * mean_out) * per_out_1, 0.1)
            fold = mean_in - mean_out
            t = fold / jnp.sqrt(var_in * per_in + var_out * per_out)
            cols = pl.ds((starts[j] + s) * LANES, LANES)
            row[:, 0, :, cols] = t.reshape(own, 1, LANES)
            row[:, 1, :, cols] = fold.reshape(own, 1, LANES)
        if j not in ROWS_AFTER:
            return
        end = starts[j] + slabs[j]
        cols = pl.ds(rows_from[0] * LANES, (end - rows_from[0]) * LANES)
        rows_from[0] = end
        for far in sorted(range(own // NY), key=lambda d: -min(d, own // NY - d)):

            for d in range(0 if far else 1, NY):
                to = peers[far, d]
                remote(row.at[to, :, :, cols], y_ref.at[g, :, :, cols], row_send, row_recv, at_genes(to))

        pltpu.make_async_copy(row.at[g, :, :, cols], y_ref.at[g, :, :, cols], row_recv).start()

    def count():
        arrived(lab.at[pl.ds(0, 2 * CHIPS - 1)], lab_recv)
        mine = lax.broadcasted_iota(jnp.int32, (own, LANES), 0) + me * own
        counts = jnp.zeros((own, LANES), jnp.float32)
        for d in range(2 * CHIPS):
            for r in range(lab_rows):
                counts += (mine == lab[d, r:r + 1, :]).astype(jnp.float32)
        return jnp.sum(counts, axis=1, keepdims=True)

    def begin(j):
        loads[j].wait()
        compute(j)
        if j == 0:
            pl.semaphore_wait(barrier, 2 * CHIPS - 1 + own - 1)
        share(j)

    begin(0)
    for d in range(1, 2 * CHIPS):
        remote(labels_ref, lab.at[me], lab_send, lab_recv, at_cells((me + d) % (2 * CHIPS)))
    lab[me] = labels_ref[...]
    begin(1)
    start_x(0)
    early_x(0)
    sizes = None
    for j in range(n):
        if j + 2 < n:
            begin(j + 2)
        if j + 1 < n:
            start_x(j + 1)
        if EAGER and j + 1 < n:
            early_x(j + 1)
        forward_x(j)
        if not EAGER and j + 1 < n:
            early_x(j + 1)
        if sizes is None:
            sizes = count()
        if j >= LAG:
            finish(j - LAG)
    for j in range(n - LAG, n):
        finish(j)

    arrived(part.at[0], pair_send)
    arrived(part.at[0, pl.ds(0, 3)], x_send)
    arrived(tot_own, tot_send)
    arrived(tot_chip.at[:, pl.ds(0, 3)], all_send)
    arrived(lab.at[pl.ds(0, 2 * CHIPS - 1)], lab_send)
    arrived(row.at[pl.ds(0, own - 1)], row_send)
    arrived(y_ref, row_recv)


def split(y_ref, t_ref, f_ref, sem):
    copies = [pltpu.make_async_copy(y_ref.at[:, kind], out, sem.at[kind]) for kind, out in enumerate((t_ref, f_ref))]
    for copy in copies:
        copy.start()
    for copy in copies:
        copy.wait()


def on_device(slabs, clusters, expression, labels):
    cell_dev, genes = expression.shape
    own = lax.axis_size("genes")
    n = len(slabs)
    f32 = jnp.float32
    rows = sum(slabs) * own
    spans = -(-sum(slabs) // SPAN)
    dma = pltpu.SemaphoreType.DMA
    y = pl.pallas_call(
        functools.partial(kernel, slabs),
        out_shape=jax.ShapeDtypeStruct((own, 2, 1, genes), f32),
        in_specs=[pl.BlockSpec(memory_space=pltpu.VMEM), pl.BlockSpec(memory_space=pl.ANY)],
        out_specs=pl.BlockSpec(memory_space=pl.ANY),
        scratch_shapes=[
            pltpu.VMEM((cell_dev, genes), jnp.bfloat16),
            pltpu.VMEM((clusters + EXTRA, cell_dev), jnp.bfloat16),
            pltpu.VMEM((2 * CHIPS, cell_dev // LANES, LANES), jnp.int32),
            pltpu.VMEM((own, 2, 1, genes), f32),
            pltpu.VMEM((spans, 2 * SPAN, LANES), f32),
            pltpu.VMEM((spans, 2 * SPAN, LANES), f32),
            pltpu.VMEM((spans, CHIPS, 2 * SPAN, LANES), f32),
            pltpu.VMEM((2, CHIPS, 2, rows, LANES), f32),
            pltpu.VMEM((CHIPS, 2, rows, LANES), f32),
            pltpu.VMEM((2, rows, LANES), f32),
            pltpu.VMEM((2, 2, rows, LANES), f32),
            dma((n,)), dma((n,)), dma((n,)), dma((n,)), dma((spans,)), dma((spans,)),
            dma, dma, dma, dma, dma, dma, dma, dma,
        ],
        compiler_params=pltpu.CompilerParams(
            collective_id=0, has_side_effects=True, vmem_limit_bytes=56 * 1024 * 1024
        ),
    )(labels.reshape(cell_dev // LANES, LANES), expression)
    line = jax.ShapeDtypeStruct((own, 1, genes), f32)
    t, fold = pl.pallas_call(
        split,
        out_shape=(line, line),
        in_specs=[pl.BlockSpec(memory_space=pltpu.VMEM)],
        out_specs=(pl.BlockSpec(memory_space=pl.ANY),) * 2,
        scratch_shapes=[dma((2,))],
    )(y)
    return t.reshape(1, own * genes), fold.reshape(1, own * genes)


def solution(mesh):
    clusters = mesh.shape["cells"] * mesh.shape["genes"]
    return jax.shard_map(
        functools.partial(on_device, SLABS, clusters),
        mesh=mesh,
        in_specs=(P("cells", "genes"), P("cells")),
        out_specs=(P(("cells", "genes"), None), P(("cells", "genes"), None)),
        check_vma=False,
    )
```

time: 44.7 us -> 41.6 us (0.931); the launches traced: 44 us -> 41.4 us
  local copies, waits for them, and re-layouts: 3.31 us -> 0 us
  Pallas kernels: 40.1 us -> 40.8 us
    unnamed x2 -> x0, local copies, waits for them, and re-layouts: 3.31 us -> none
    pallas_call x1 -> x2, Pallas kernels: 40.1 us -> 40.8 us  [the longest x1 39 us: on_device(): pl.pallas_call(functools.partial(kernel, slabs), out_shape=jax.ShapeDtype...]
where the time goes in v2:
time: 41.6 us; the launch traced here: 41.4 us
  Pallas kernels  40.8 us (98%)
  between operations  0.64 us (2%)
    pallas_call x1, Pallas kernels, on_device(): pl.pallas_call(functools.partial(kernel, slabs), out_shape=jax.ShapeDtype...  39 us
    pallas_call x1, Pallas kernels, on_device(): pl.pallas_call(split, out_shape=(line, line), in_specs=[pl.BlockSpec(memo...  1.82 us

profile of v2, /device:TPU:1, one launch (start us, length us, event | category | flops | bytes accessed | tf_op | source)
XLA Modules:
  0.0 41.4 jit_solution(382138784803675392)
XLA Ops:
  0.6 39.0 %shard_map.41.y_ref = f32[32,2,1,1920]{3,2,1,0:T(1,128)} custom-call(s32[16,128]{1,0:T(8,128)} %bitcast.3, bf16[2048,1920]{1,0:T(8,128)(2,1)} %x_ref.1), custom_call_target="tpu_custom_call" | custom-call | tf_op jit(solution)/shard_map/pallas_call | solution.py:245
  39.6 1.8 %shard_map.42 = (f32[32,1,1920]{2,1,0:T(1,128)}, f32[32,1,1920]{2,1,0:T(1,128)}) custom-call(f32[32,2,1,1920]{3,2,1,0:T(1,128)} %shard_map.41.y_ref), custom_call_target="tpu_custom_call" | custom-call | tf_op jit(solution)/shard_map/pallas_call | solution.py:270

commit v3 on v2

--- a/solution.py
+++ b/solution.py
@@ -10,21 +10,26 @@
 MESH = pl.DeviceIdType.MESH
 LANES = 128
 CHIPS = 4
-SLABS = (4, 4, 4, 3)
+SLABS = (4, 4, 3, 2, 2)
 NY = 4
+PIECES = 4
 EXTRA = 16
-EAGER, LAG = False, 1
+ORDER = (
+    "b0", "b1", "s0", "e0", "b2", "s1", "b3", "e1", "f0", "b4",
+    "s2", "f1", "s3", "s4", "e2", "n0", "f2", "e3", "n1", "f3",
+    "e4", "f4", "n2", "n3", "n4",
+)
 SPAN = 4
-ROWS_AFTER = (0, 1, 2, 3)
+ROWS_AFTER = (0, 1, 2, 3, 4)
 
 
 def kernel(slabs, labels_ref, x_ref, y_ref, xv, member, lab, row, tot_own, tot_pair, tot_chip,
            part, pair, hop, final, load_sem, pair_recv, hop_recv, final_recv, tot_recv, all_recv,
-           pair_send, x_send, tot_send, all_send, lab_send, lab_recv, row_send, row_recv):
+           pair_send, x_send, tot_send, all_send, lab_send, lab_recv, row_send, row_recv, label_sem):
     n = len(slabs)
     starts = [sum(slabs[:j]) for j in range(n)]
     clusters, cell_dev = member.shape[0] - EXTRA, member.shape[1]
-    lab_rows = labels_ref.shape[0]
+    lab_rows = lab.shape[1]
     own = row.shape[0]
     cells_all = jnp.float32(cell_dev * 2 * CHIPS)
 
@@ -39,11 +44,14 @@
     def at_genes(index):
         return {"cells": me, "genes": index}
 
+    own_labels = pltpu.make_async_copy(labels_ref, lab.at[lax.axis_index("cells")], label_sem)
+    own_labels.start()
     loads = []
     for j in range(n):
         cols = pl.ds(starts[j] * LANES, slabs[j] * LANES)
         loads.append(pltpu.make_async_copy(x_ref.at[:, cols], xv.at[:, cols], load_sem.at[j]))
-        loads[j].start()
+        if j == 0:
+            loads[j].start()
 
     barrier = pltpu.get_barrier_semaphore()
     for d in range(1, 2 * CHIPS):
@@ -57,8 +65,9 @@
             pl.semaphore_signal(barrier, inc=1, device_id=at_genes(peers[far, d]), device_id_type=MESH)
 
     ids = lax.broadcasted_iota(jnp.int32, (clusters, LANES), 0)
+    own_labels.wait()
     for r in range(cell_dev // LANES):
-        hits = (ids == labels_ref[r:r + 1, :]).astype(jnp.float32).astype(jnp.bfloat16)
+        hits = (ids == lab[me, r:r + 1, :]).astype(jnp.float32).astype(jnp.bfloat16)
         member[:clusters, r * LANES:(r + 1) * LANES] = hits
     member[clusters:, :] = jnp.ones((EXTRA, cell_dev), jnp.bfloat16)
     tot_own[...] = jnp.zeros_like(tot_own)
@@ -187,35 +196,23 @@
 
     def begin(j):
         loads[j].wait()
+        if j == 0:
+            for load in loads[1:]:
+                load.start()
         compute(j)
         if j == 0:
             pl.semaphore_wait(barrier, 2 * CHIPS - 1 + own - 1)
         share(j)
-
-    begin(0)
-    for d in range(1, 2 * CHIPS):
-        remote(labels_ref, lab.at[me], lab_send, lab_recv, at_cells((me + d) % (2 * CHIPS)))
-    lab[me] = labels_ref[...]
-    begin(1)
-    start_x(0)
-    early_x(0)
+        if j == 0:
+            for d in range(1, 2 * CHIPS):
+                remote(lab.at[me], lab.at[me], lab_send, lab_recv, at_cells((me + d) % (2 * CHIPS)))
+
+    steps = {"b": begin, "s": start_x, "e": early_x, "f": forward_x, "n": finish}
     sizes = None
-    for j in range(n):
-        if j + 2 < n:
-            begin(j + 2)
-        if j + 1 < n:
-            start_x(j + 1)
-        if EAGER and j + 1 < n:
-            early_x(j + 1)
-        forward_x(j)
-        if not EAGER and j + 1 < n:
-            early_x(j + 1)
-        if sizes is None:
+    for step in ORDER:
+        if step[0] == "n" and sizes is None:
             sizes = count()
-        if j >= LAG:
-            finish(j - LAG)
-    for j in range(n - LAG, n):
-        finish(j)
+        steps[step[0]](int(step[1]))
 
     arrived(part.at[0], pair_send)
     arrived(part.at[0, pl.ds(0, 3)], x_send)
@@ -226,12 +223,20 @@
     arrived(y_ref, row_recv)
 
 
-def split(y_ref, t_ref, f_ref, sem):
-    copies = [pltpu.make_async_copy(y_ref.at[:, kind], out, sem.at[kind]) for kind, out in enumerate((t_ref, f_ref))]
-    for copy in copies:
-        copy.start()
-    for copy in copies:
-        copy.wait()
+def split(y_ref, t_ref, f_ref, held, in_sem, out_sem):
+    step = held.shape[0] // PIECES
+    pieces = [pl.ds(i * step, step) for i in range(PIECES)]
+    loads = [pltpu.make_async_copy(y_ref.at[p], held.at[p], in_sem.at[i]) for i, p in enumerate(pieces)]
+    for load in loads:
+        load.start()
+    stores = []
+    for i, p in enumerate(pieces):
+        loads[i].wait()
+        for kind, out in enumerate((t_ref, f_ref)):
+            stores.append(pltpu.make_async_copy(held.at[p, kind], out.at[p], out_sem.at[i, kind]))
+            stores[-1].start()
+    for store in stores:
+        store.wait()
 
 
 def on_device(slabs, clusters, expression, labels):
@@ -245,7 +250,7 @@
     y = pl.pallas_call(
         functools.partial(kernel, slabs),
         out_shape=jax.ShapeDtypeStruct((own, 2, 1, genes), f32),
-        in_specs=[pl.BlockSpec(memory_space=pltpu.VMEM), pl.BlockSpec(memory_space=pl.ANY)],
+        in_specs=[pl.BlockSpec(memory_space=pltpu.HBM), pl.BlockSpec(memory_space=pl.ANY)],
         out_specs=pl.BlockSpec(memory_space=pl.ANY),
         scratch_shapes=[
             pltpu.VMEM((cell_dev, genes), jnp.bfloat16),
@@ -260,7 +265,7 @@
             pltpu.VMEM((2, rows, LANES), f32),
             pltpu.VMEM((2, 2, rows, LANES), f32),
             dma((n,)), dma((n,)), dma((n,)), dma((n,)), dma((spans,)), dma((spans,)),
-            dma, dma, dma, dma, dma, dma, dma, dma,
+            dma, dma, dma, dma, dma, dma, dma, dma, dma,
         ],
         compiler_params=pltpu.CompilerParams(
             collective_id=0, has_side_effects=True, vmem_limit_bytes=56 * 1024 * 1024
@@ -270,9 +275,9 @@
     t, fold = pl.pallas_call(
         split,
         out_shape=(line, line),
-        in_specs=[pl.BlockSpec(memory_space=pltpu.VMEM)],
+        in_specs=[pl.BlockSpec(memory_space=pltpu.HBM)],
         out_specs=(pl.BlockSpec(memory_space=pl.ANY),) * 2,
-        scratch_shapes=[dma((2,))],
+        scratch_shapes=[pltpu.VMEM((own, 2, 1, genes), f32), dma((PIECES,)), dma((PIECES, 2))],
     )(y)
     return t.reshape(1, own * genes), fold.reshape(1, own * genes)
 

time: 41.6 us -> 40.6 us (0.976)
  Pallas kernels: 40.8 us -> 39.8 us
    pallas_call x1, Pallas kernels: 39 us -> 38 us  [on_device(): pl.pallas_call(functools.partial(kernel, slabs), out_shape=jax.ShapeDtype...]
where the time goes in v3:
time: 40.6 us; the launch traced here: 40.4 us
  Pallas kernels  39.8 us (98%)
  between operations  0.64 us (2%)
    pallas_call x1, Pallas kernels, on_device(): pl.pallas_call(functools.partial(kernel, slabs), out_shape=jax.ShapeDtype...  38 us
    pallas_call x1, Pallas kernels, on_device(): pl.pallas_call(split, out_shape=(line, line), in_specs=[pl.BlockSpec(memo...  1.83 us

profile of v3, /device:TPU:1, one launch (start us, length us, event | category | flops | bytes accessed | tf_op | source)
XLA Modules:
  0.0 40.4 jit_solution(11528071676423226062)
XLA Ops:
  0.6 38.0 %shard_map.41.y_ref = f32[32,2,1,1920]{3,2,1,0:T(1,128)} custom-call(s32[16,128]{1,0:T(8,128)} %bitcast.3, bf16[2048,1920]{1,0:T(8,128)(2,1)} %x_ref.1), custom_call_target="tpu_custom_call" | custom-call | tf_op jit(solution)/shard_map/pallas_call | solution.py:250
  38.6 1.8 %shard_map.42 = (f32[32,1,1920]{2,1,0:T(1,128)}, f32[32,1,1920]{2,1,0:T(1,128)}) custom-call(f32[32,2,1,1920]{3,2,1,0:T(1,128)} %shard_map.41.y_ref), custom_call_target="tpu_custom_call" | custom-call | tf_op jit(solution)/shard_map/pallas_call | solution.py:275

commit v4 on v3

--- a/solution.py
+++ b/solution.py
@@ -15,7 +15,7 @@
 PIECES = 4
 EXTRA = 16
 ORDER = (
-    "b0", "b1", "s0", "e0", "b2", "s1", "b3", "e1", "f0", "b4",
+    "b0", "c0", "b1", "s0", "e0", "c1", "b2", "c2", "s1", "b3", "e1", "f0", "b4",
     "s2", "f1", "s3", "s4", "e2", "n0", "f2", "e3", "n1", "f3",
     "e4", "f4", "n2", "n3", "n4",
 )
@@ -75,8 +75,8 @@
     def rows_of(j):
         return pl.ds(starts[j] * own, slabs[j] * own)
 
-    def compute(j):
-        for s0 in range(0, slabs[j], 2):
+    def compute(j, blocks):
+        for s0 in blocks:
             width = min(2, slabs[j] - s0)
             base = starts[j] + s0
             x = xv[:, base * LANES:(base + width) * LANES]
@@ -111,11 +111,11 @@
         j = max(j for j in range(n) if starts[j] <= last)
         spans.setdefault(j, []).append(span)
 
-    def share(j):
+    def share(j, first, last):
         partner = at_cells(2 * chip + 1 - core)
-        rows = rows_of(j)
+        rows = pl.ds((starts[j] + first) * own, (last - first) * own)
         remote(part.at[1 - core, :, :, rows], pair.at[:, :, rows], pair_send, pair_recv.at[j], partner)
-        for span in spans.get(j, ()):
+        for span in spans.get(j, ()) if last == slabs[j] else ():
             remote(tot_own.at[span], tot_pair.at[span], tot_send, tot_recv.at[span], partner)
 
     def start_x(j):
@@ -199,15 +199,19 @@
         if j == 0:
             for load in loads[1:]:
                 load.start()
-        compute(j)
+        compute(j, (0,))
         if j == 0:
             pl.semaphore_wait(barrier, 2 * CHIPS - 1 + own - 1)
-        share(j)
+        share(j, 0, min(2, slabs[j]))
         if j == 0:
             for d in range(1, 2 * CHIPS):
                 remote(lab.at[me], lab.at[me], lab_send, lab_recv, at_cells((me + d) % (2 * CHIPS)))
 
-    steps = {"b": begin, "s": start_x, "e": early_x, "f": forward_x, "n": finish}
+    def rest(j):
+        compute(j, range(2, slabs[j], 2))
+        share(j, 2, slabs[j])
+
+    steps = {"b": begin, "c": rest, "s": start_x, "e": early_x, "f": forward_x, "n": finish}
     sizes = None
     for step in ORDER:
         if step[0] == "n" and sizes is None:

time: 40.6 us -> 44.8 us (1.10)
  Pallas kernels: 39.8 us -> 44 us
    pallas_call x1, Pallas kernels: 38 us -> 42.2 us  [on_device(): pl.pallas_call(functools.partial(kernel, slabs), out_shape=jax.ShapeDtype...]
where the time goes in v4:
time: 44.8 us; the launch traced here: 44.7 us
  Pallas kernels  44 us (98%)
  between operations  0.64 us (1%)
    pallas_call x1, Pallas kernels, on_device(): pl.pallas_call(functools.partial(kernel, slabs), out_shape=jax.ShapeDtype...  42.2 us
    pallas_call x1, Pallas kernels, on_device(): pl.pallas_call(split, out_shape=(line, line), in_specs=[pl.BlockSpec(memo...  1.83 us

profile of v4, /device:TPU:1, one launch (start us, length us, event | category | flops | bytes accessed | tf_op | source)
XLA Modules:
  0.0 44.7 jit_solution(3486718921879445434)
XLA Ops:
  0.6 42.2 %shard_map.41.y_ref = f32[32,2,1,1920]{3,2,1,0:T(1,128)} custom-call(s32[16,128]{1,0:T(8,128)} %bitcast.3, bf16[2048,1920]{1,0:T(8,128)(2,1)} %x_ref.1), custom_call_target="tpu_custom_call" | custom-call | tf_op jit(solution)/shard_map/pallas_call | solution.py:254
  42.8 1.8 %shard_map.42 = (f32[32,1,1920]{2,1,0:T(1,128)}, f32[32,1,1920]{2,1,0:T(1,128)}) custom-call(f32[32,2,1,1920]{3,2,1,0:T(1,128)} %shard_map.41.y_ref), custom_call_target="tpu_custom_call" | custom-call | tf_op jit(solution)/shard_map/pallas_call | solution.py:279
